TPU v7x, 512 devices: a whole 4x8x8 slice. The times are simulated.
512 devices in a mesh: tm: 16 (over y, core), nin: 8 (over z), nout: 4 (over x).
Axes of the slice: x: 4, y: 8, z: 8, core: 2. Of those that a mesh axis runs over, the one named last changes fastest.
Arguments:
- spikes: int32 [4096, 2048], P('tm', 'nin'), may hold values 0 or 1
- exposure: int32 [4096], P('tm'), may hold values from 1 to 8
- weights: bfloat16 [16384, 2048], P('nin', 'nout'), may hold values from -0.375 to 0.375
- direction: float32 [16384, 2048], P(('nin', 'tm'), 'nout'), may hold values from -6 to 6
- residual: float32 [16384, 2048], P(('nin', 'tm'), 'nout'), may hold values from -0.75 to 0.75
- iterate: float32 [16384, 2048], P(('nin', 'tm'), 'nout'), may hold values from -1.8 to 1.8
Outputs:
- new_iterate: float32 [16384, 2048], P(('nin', 'tm'), 'nout')
- new_residual: float32 [16384, 2048], P(('nin', 'tm'), 'nout')
- new_direction: float32 [16384, 2048], P(('nin', 'tm'), 'nout')
All inputs are finite; a program needn't handle non-finite values. No bound on the sum of `spikes` on one device may be relied on, other than what follows from the above.
Results may differ from a plain program's by a relative error of at most 0.015.
Values may be sent and summed in bfloat16 or wider, within the bound.
A program may use at most 64 MiB of HBM per device.

v0:
```python
import math
import jax
import jax.numpy as jnp
from jax import lax
from jax.sharding import PartitionSpec as P

BASES = 8
HISTORY = 128
RIDGE_WEIGHT = 0.05
NORM_EPS = 1e-06


def shifted(value, axis, steps):
    count = lax.axis_size(axis)
    initial, last = (max(0, -steps), min(count, count - steps))
    return lax.ppermute(value, axis, [(source, source + steps) for source in range(initial, last)])


def basis_table(history, bases_count):
    lag_values = jnp.arange(1, history + 1, dtype=jnp.float32)
    warped = jnp.log(lag_values + 1.0)
    log_low = math.log(2.0)
    log_high = math.log(history + 1.0)
    spacing = (log_high - log_low) / (bases_count - 1)
    centers = log_low + spacing * jnp.arange(bases_count, dtype=jnp.float32)
    phases = (warped[:, None] - centers[None, :]) * (math.pi / (2.0 * spacing))
    phases = jnp.clip(phases, -math.pi, math.pi)
    bump_values = 0.5 * (1.0 + jnp.cos(phases))
    bump_values = bump_values / jnp.sum(bump_values, axis=0, keepdims=True)
    return bump_values.astype(jnp.bfloat16)


def lag_kernel(basis_rows, span, offset):
    out_index = jnp.arange(span, dtype=jnp.int32)[:, None]
    in_index = jnp.arange(span, dtype=jnp.int32)[None, :]
    lag_index = out_index + offset - in_index
    is_valid = (lag_index >= 1) & (lag_index <= HISTORY)
    take_index = jnp.clip(lag_index - 1, 0, HISTORY - 1)
    return jnp.where(
        is_valid[None], jnp.take(basis_rows.T, take_index, axis=1), jnp.zeros((), jnp.bfloat16)
    )


def per_device(spikes, exposure, weights, direction, residual, iterate):
    block_rows = spikes.shape[0]
    neuron_cols = spikes.shape[1]
    basis_rows = basis_table(HISTORY, BASES)
    spike_low = spikes.astype(jnp.bfloat16)
    block_count = block_rows // HISTORY
    stacked = spike_low.reshape(block_count, HISTORY, neuron_cols)
    kernel_same = lag_kernel(basis_rows, HISTORY, 0)
    kernel_before = lag_kernel(basis_rows, HISTORY, HISTORY)
    current = jnp.einsum("bim,cmn->cinb", kernel_same, stacked, preferred_element_type=jnp.float32)
    tail_part = jnp.einsum(
        "bim,mn->inb", kernel_before, stacked[-1], preferred_element_type=jnp.float32
    )
    inner_part = jnp.einsum(
        "bim,cmn->cinb", kernel_before, stacked[:-1], preferred_element_type=jnp.float32
    )
    tail_terms = shifted(tail_part.astype(jnp.bfloat16), "tm", 1).astype(tail_part.dtype)
    own_terms = current + jnp.concatenate([tail_terms[None], inner_part], axis=0)
    features = own_terms.reshape(block_rows, neuron_cols * BASES).astype(jnp.bfloat16)
    direction_low = direction.astype(jnp.bfloat16)
    columns = features
    along_part = jnp.dot(
        columns,
        lax.all_gather(direction_low, "tm", axis=0, tiled=True),
        preferred_element_type=jnp.float32,
    )
    predictor_part = jnp.dot(features, weights, preferred_element_type=jnp.float32)
    tick_scale = exposure.astype(jnp.float32) / 8.0
    predictor_full, along_full = (
        lax.psum(predictor_part.astype(jnp.bfloat16), "nin").astype(jnp.float32),
        lax.psum(along_part.astype(jnp.bfloat16), "nin").astype(jnp.float32),
    )
    weighted = (tick_scale[:, None] * jnp.exp(predictor_full) * along_full).astype(jnp.bfloat16)
    columns = features
    gram = lax.psum_scatter(
        lax.dot_general(
            columns, weighted, (((0,), (0,)), ((), ())), preferred_element_type=jnp.float32
        ).astype(jnp.bfloat16),
        "tm",
        scatter_dimension=0,
        tiled=True,
    ).astype(jnp.float32)
    bin_total = block_rows * lax.axis_size("tm")
    curvature_prod = gram / bin_total + RIDGE_WEIGHT * direction
    old_norm, curvature = lax.psum(
        (jnp.sum(residual * residual, axis=0), jnp.sum(direction * curvature_prod, axis=0)),
        ("tm", "nin"),
    )
    step_size = old_norm / curvature
    new_iterate = iterate + step_size[None, :] * direction
    new_residual = residual - step_size[None, :] * curvature_prod
    new_norm = lax.psum(jnp.sum(new_residual * new_residual, axis=0), ("tm", "nin"))
    new_direction = new_residual + (new_norm / (old_norm + NORM_EPS))[None, :] * direction
    return (new_iterate, new_residual, new_direction)


def solution(mesh):
    in_specs = (
        P("tm", "nin"),
        P("tm"),
        P("nin", "nout"),
        P(("nin", "tm"), "nout"),
        P(("nin", "tm"), "nout"),
        P(("nin", "tm"), "nout"),
    )
    out_specs = (P(("nin", "tm"), "nout"), P(("nin", "tm"), "nout"), P(("nin", "tm"), "nout"))
    return jax.shard_map(
        per_device, mesh=mesh, in_specs=in_specs, out_specs=out_specs, check_vma=False
    )
```

profile of v0, /device:TPU:2, one launch (start us, length us, event | category | flops | bytes accessed | tf_op | source)
XLA Modules:
  0.0 800.1 jit_solution(18235166921538115580)
XLA Ops:
  7.2 0.0 all-gather.2.cloned.1.call-start
  7.2 1.8 convert_element_type.56
  9.0 0.0 all-gather.2.cloned.1.call-update
  9.0 0.0 all-reduce.4.cloned.1.call-start
  9.1 0.2 multiply_reduce_fusion.3
  9.3 0.1 divide_convert_fusion
  9.4 0.1 copy.17
  9.6 0.1 bitcast_clamp_fusion
  9.7 57.8 %gather_fusion.1 = bf16[16384,8]{1,0:T(8,128)(2,1)} fusion(bf16[8,128]{0,1:T(8,128)(2,1)S(1)} %copy.17, s32[16384]{0:T(1024)S(1)} %bitcast_clamp_fusion), kind=kCustom, calls=%fused_computation.1.clone | custom fusion | bytes 589824 | tf_op jit(solution)/shard_map/jit(_take)/gather | solution.py:40
  67.5 3.6 copy.20
  71.2 0.1 fusion.30
  71.3 1.1 fusion.1
  72.4 1.8 collective-permute-start
  74.2 57.8 %gather_fusion = bf16[16384,8]{1,0:T(8,128)(2,1)} fusion(bf16[8,128]{0,1:T(8,128)(2,1)S(1)} %copy.17, s32[16384]{0:T(1024)S(1)} %bitcast_clamp_fusion.1), kind=kCustom, calls=%fused_computation.clone | custom fusion | bytes 589824 | tf_op jit(solution)/shard_map/jit(_take)/gather | solution.py:40
  132.0 3.6 copy.18
  135.6 0.1 fusion.27
  135.7 0.3 convolution_bitcast_fusion
  136.0 0.1 bitcast_convert_fusion
  136.1 0.4 fusion
  136.5 2.1 copy.21
  138.6 2.8 convolution_convert_fusion.3
  141.4 3.0 convolution_convert_fusion.2
  144.4 0.0 all-reduce.4.cloned.1.call-update
  144.5 0.0 reduce-scatter.2.cloned.1.call-start
  144.5 85.0 %all-reduce.4.cloned.1.call-done = (bf16[256,512]{1,0:T(8,128)(2,1)}, bf16[256,512]{1,0:T(8,128)(2,1)}) async-done(((bf16[256,512]{1,0:T(8,128)(2,1)}, bf16[256,512]{1,0:T(8,128)(2,1)}), (bf16[256,512]{1,0:T(8,128)(2,1)}, bf16[256,512]{1,0:T(8,128)(2,1)})) %all-reduce.4.cloned.1.call-update) | async-done | bytes 524304 | tf_op jit(solution)/shard_map/psum | solution.py:74
  229.5 3.2 convolution_convert_fusion
  232.9 59.8 %reduce-scatter.2.cloned.1.call-done = bf16[128,512]{1,0:T(8,128)(2,1)} async-done(((bf16[2048,512]{1,0:T(8,128)(2,1)}), bf16[128,512]{1,0:T(8,128)(2,1)}) %reduce-scatter.2.cloned.1.call-update) | async-done | bytes 131088 | tf_op jit(solution)/shard_map/reduce_scatter | solution.py:78
  292.7 1.0 multiply_reduce_fusion.1
  293.6 250.6 %all-reduce = (f32[512]{0:T(512)S(1)}, f32[512]{0:T(512)S(1)}) all-reduce(f32[512]{0:T(512)S(1)} %multiply_reduce_fusion.2, f32[512]{0:T(512)S(1)} %multiply_reduce_fusion.1), channel_id=1, replica_groups=mesh['tm'=16,'nin'=8,'nout'=4] {'tm','nin'}, use_global_device_ids=true, to_apply=%region_1.2 | all-reduce | flops 1024 | bytes 8192 | tf_op jit(solution)/shard_map/psum | solution.py:88
  544.3 1.7 multiply_reduce_fusion
  546.0 246.8 %psum.39 = f32[512]{0:T(512)S(1)} all-reduce(f32[512]{0:T(512)S(1)} %get-tuple-element.8), channel_id=1, replica_groups=mesh['tm'=16,'nin'=8,'nout'=4] {'tm','nin'}, use_global_device_ids=true, to_apply=%region_9.11 | all-reduce | flops 512 | bytes 4096 | tf_op jit(solution)/shard_map/psum | solution.py:95
  792.8 0.8 multiply_add_fusion
  (28 shorter events, 0.2 us)
Async XLA Ops:
  7.2 131.5 %copy-start = (bf16[2048,512]{1,0:T(8,128)(2,1)S(1)}, bf16[2048,512]{1,0:T(8,128)(2,1)}, u32[]{:S(2)}) copy-start(bf16[2048,512]{1,0:T(8,128)(2,1)} %param.10) | copy-start | bytes 6291460
  7.2 134.2 %all-gather.2.cloned.1.call-start = ((), (), s32[]{:S(2)}) async-start(), calls=%async_computation.1 | async-start | bytes 2228224 | tf_op jit(solution)/shard_map/all_gather | solution.py:67
  9.0 220.5 %all-reduce.4.cloned.1.call-start = ((), (), s32[]{:S(2)}) async-start(), calls=%async_computation.3 | async-start | bytes 1048576 | tf_op jit(solution)/shard_map/psum | solution.py:74
  67.5 3.6 copy-start.5
  72.4 63.6 %collective-permute-start = (bf16[128,256,8]{1,0,2:T(8,128)(2,1)}, bf16[128,256,8]{1,0,2:T(8,128)(2,1)S(1)}, u32[]{:S(2)}, u32[]{:S(2)}) collective-permute-start(bf16[128,256,8]{1,0,2:T(8,128)(2,1)} %fusion.1), channel_id=1, source_target_pairs={{0,32},{32,64},{64,96},{96,128},{128,160},{160,192},{192,224},{224... | collective-permute-start | bytes 1572872 | tf_op jit(solution)/shard_map/ppermute | solution.py:16
  138.6 2.8 copy-start.2
  141.4 3.1 copy-start.7
  144.5 148.2 %reduce-scatter.2.cloned.1.call-start = ((), (), s32[]{:S(2)}) async-start(), calls=%async_computation.2 | async-start | bytes 2228224 | tf_op jit(solution)/shard_map/reduce_scatter | solution.py:78
  229.5 3.3 copy-start.4
  232.8 59.9 %copy-start.1 = (f32[128,512]{1,0:T(8,128)S(1)}, f32[128,512]{1,0:T(8,128)}, u32[]{:S(2)}) copy-start(f32[128,512]{1,0:T(8,128)} %param.11) | copy-start | bytes 786436
  232.8 311.5 %copy-start.6 = (f32[128,512]{1,0:T(8,128)S(1)}, f32[128,512]{1,0:T(8,128)}, u32[]{:S(2)}) copy-start(f32[128,512]{1,0:T(8,128)} %param.13) | copy-start | bytes 786436
  546.0 247.6 %copy-start.3 = (f32[128,512]{1,0:T(8,128)}, f32[128,512]{1,0:T(8,128)S(1)}, u32[]{:S(2)}) copy-start(f32[128,512]{1,0:T(8,128)S(1)} %get-tuple-element.9) | copy-start | bytes 786436
Sparse Core Ops, SparseCore 0:
  10.7 46.5 all-gather.1
  144.6 84.9 all-reduce.3
  232.9 59.6 reduce-scatter.1
where the time goes:
time: 800 us
  blocking collectives  497 us (62%)
  waiting for transfers between devices  145 us (18%)
  local copies, waits for them, and re-layouts  125 us (16%)
  between operations  13.9 us (2%)
  matrix products  10.8 us (1%)
    psum x1, blocking collectives, per_device(): lax.psum((jnp.sum(residual * residual, axis=0), jnp.sum(direction * curva...  251 us
    psum x1, blocking collectives, per_device(): lax.psum(jnp.sum(new_residual * new_residual, axis=0), ('tm', 'nin'))  247 us
    gather x4, local copies, waits for them, and re-layouts, lag_kernel(): jnp.take(basis_rows.T, take_index, axis=1)  123 us
    psum x1, waiting for transfers between devices, per_device(): lax.psum(along_part.astype(jnp.bfloat16), 'nin').astype(jnp.float32)  85 us
    reduce_scatter x1, waiting for transfers between devices, per_device(): lax.psum_scatter(lax.dot_general(columns, weighted, (((0,), (0,)), ((), (...  59.8 us
  transfers between devices with their start and end apart: 4, of which 2 were waited for; matrix products, arithmetic and copies ran while one was open for 16% of the time, Pallas kernels for 0%

commit v1 on v0

--- a/solution.py
+++ b/solution.py
@@ -86,8 +86,11 @@
     bin_total = block_rows * lax.axis_size("tm")
     curvature_prod = gram / bin_total + RIDGE_WEIGHT * direction
     old_norm, curvature = lax.psum(
-        (jnp.sum(residual * residual, axis=0), jnp.sum(direction * curvature_prod, axis=0)),
-        ("tm", "nin"),
+        lax.psum(
+            (jnp.sum(residual * residual, axis=0), jnp.sum(direction * curvature_prod, axis=0)),
+            "nin",
+        ),
+        "tm",
     )
     step_size = old_norm / curvature
     new_iterate = iterate + step_size[None, :] * direction

time: 800 us -> 591 us (0.74)
  blocking collectives: 497 us -> 288 us
    psum x1, blocking collectives: 251 us -> 18.1 us  [per_device(): lax.psum((jnp.sum(residual * residual, axis=0), jnp.sum(direction * curva...]
    psum x0 -> x1, blocking collectives: none -> 23.5 us  [per_device(): lax.psum(lax.psum((jnp.sum(residual * residual, axis=0), jnp.sum(directio...]
  transfers between devices with their start and end apart: 4 -> 4, of which waited for: 2 -> 2; matrix products, arithmetic and copies ran while one was open for 16% -> 22% of each run, Pallas kernels for 0% -> 0%
where the time goes in v1:
time: 591 us; the launch traced here: 590 us
  blocking collectives  288 us (49%)
  waiting for transfers between devices  145 us (25%)
  local copies, waits for them, and re-layouts  124 us (21%)
  between operations  13.9 us (2%)
  matrix products  10.8 us (2%)
  other arithmetic  6.02 us (1%)
    psum x1, blocking collectives, per_device(): lax.psum(jnp.sum(new_residual * new_residual, axis=0), ('tm', 'nin'))  247 us
    gather x4, local copies, waits for them, and re-layouts, lag_kernel(): jnp.take(basis_rows.T, take_index, axis=1)  122 us
    psum x1, waiting for transfers between devices, per_device(): lax.psum(along_part.astype(jnp.bfloat16), 'nin').astype(jnp.float32)  85 us
    reduce_scatter x1, waiting for transfers between devices, per_device(): lax.psum_scatter(lax.dot_general(columns, weighted, (((0,), (0,)), ((), (...  59.8 us
    psum x1, blocking collectives, per_device(): lax.psum(lax.psum((jnp.sum(residual * residual, axis=0), jnp.sum(directio...  23.5 us
    psum x1, blocking collectives, per_device(): lax.psum((jnp.sum(residual * residual, axis=0), jnp.sum(direction * curva...  18.1 us
  transfers between devices with their start and end apart: 4, of which 2 were waited for; matrix products, arithmetic and copies ran while one was open for 22% of the time, Pallas kernels for 0%

profile of v1, /device:TPU:2, one launch (start us, length us, event | category | flops | bytes accessed | tf_op | source)
XLA Modules:
  0.0 590.2 jit_solution(10912039187463895162)
XLA Ops:
  7.2 0.0 all-gather.2.cloned.1.call-start
  7.2 1.8 convert_element_type.56
  9.0 0.0 all-reduce.5.cloned.1.call-start
  9.1 0.2 multiply_reduce_fusion.3
  9.3 0.1 divide_convert_fusion
  9.4 0.1 copy.17
  9.6 0.1 bitcast_clamp_fusion
  9.7 57.4 %gather_fusion.1 = bf16[16384,8]{1,0:T(8,128)(2,1)} fusion(bf16[8,128]{0,1:T(8,128)(2,1)S(1)} %copy.17, s32[16384]{0:T(1024)S(1)} %bitcast_clamp_fusion), kind=kCustom, calls=%fused_computation.1.clone | custom fusion | bytes 589824 | tf_op jit(solution)/shard_map/jit(_take)/gather | solution.py:40
  67.1 3.6 copy.20
  70.8 0.1 fusion.30
  70.9 1.1 fusion.1
  72.0 1.8 collective-permute-start
  73.8 57.4 %gather_fusion = bf16[16384,8]{1,0:T(8,128)(2,1)} fusion(bf16[8,128]{0,1:T(8,128)(2,1)S(1)} %copy.17, s32[16384]{0:T(1024)S(1)} %bitcast_clamp_fusion.1), kind=kCustom, calls=%fused_computation.clone | custom fusion | bytes 589824 | tf_op jit(solution)/shard_map/jit(_take)/gather | solution.py:40
  131.2 3.6 copy.18
  134.7 0.1 fusion.27
  134.8 0.3 convolution_bitcast_fusion
  135.1 0.1 bitcast_convert_fusion
  135.2 0.4 fusion
  135.6 2.1 copy.21
  137.7 2.8 convolution_convert_fusion.3
  140.5 3.1 convolution_convert_fusion.2
  143.6 0.0 all-reduce.5.cloned.1.call-update
  143.6 0.0 reduce-scatter.2.cloned.1.call-start
  143.6 85.0 %all-reduce.5.cloned.1.call-done = (bf16[256,512]{1,0:T(8,128)(2,1)}, bf16[256,512]{1,0:T(8,128)(2,1)}) async-done(((bf16[256,512]{1,0:T(8,128)(2,1)}, bf16[256,512]{1,0:T(8,128)(2,1)}), (bf16[256,512]{1,0:T(8,128)(2,1)}, bf16[256,512]{1,0:T(8,128)(2,1)})) %all-reduce.5.cloned.1.call-update) | async-done | bytes 524304 | tf_op jit(solution)/shard_map/psum | solution.py:74
  228.7 3.2 convolution_convert_fusion
  232.0 59.8 %reduce-scatter.2.cloned.1.call-done = bf16[128,512]{1,0:T(8,128)(2,1)} async-done(((bf16[2048,512]{1,0:T(8,128)(2,1)}), bf16[128,512]{1,0:T(8,128)(2,1)}) %reduce-scatter.2.cloned.1.call-update) | async-done | bytes 131088 | tf_op jit(solution)/shard_map/reduce_scatter | solution.py:78
  291.8 1.0 multiply_reduce_fusion.1
  292.8 18.1 %all-reduce.1 = (f32[512]{0:T(512)S(1)}, f32[512]{0:T(512)S(1)}) all-reduce(f32[512]{0:T(512)S(1)} %multiply_reduce_fusion.2, f32[512]{0:T(512)S(1)} %multiply_reduce_fusion.1), channel_id=1, replica_groups=mesh['tm'=16,'nin'=8,'nout'=4] {'nin'}, use_global_device_ids=true, to_apply=%region_1.2 | all-reduce | flops 1024 | bytes 8192 | tf_op jit(solution)/shard_map/psum | solution.py:89
  310.8 23.5 %all-reduce = (f32[512]{0:T(512)S(1)}, f32[512]{0:T(512)S(1)}) all-reduce(f32[512]{0:T(512)S(1)} %get-tuple-element.6, f32[512]{0:T(512)S(1)} %get-tuple-element.7), channel_id=1, replica_groups=mesh['tm'=16,'nin'=8,'nout'=4] {'tm'}, use_global_device_ids=true, to_apply=%region_2.3 | all-reduce | flops 1024 | bytes 8192 | tf_op jit(solution)/shard_map/psum | solution.py:88
  334.4 1.7 multiply_reduce_fusion
  336.1 246.9 %psum.55 = f32[512]{0:T(512)S(1)} all-reduce(f32[512]{0:T(512)S(1)} %get-tuple-element.10), channel_id=1, replica_groups=mesh['tm'=16,'nin'=8,'nout'=4] {'tm','nin'}, use_global_device_ids=true, to_apply=%region_11.13 | all-reduce | flops 512 | bytes 4096 | tf_op jit(solution)/shard_map/psum | solution.py:98
  583.0 0.8 multiply_add_fusion
  (29 shorter events, 0.2 us)
Async XLA Ops:
  7.2 130.6 %copy-start = (bf16[2048,512]{1,0:T(8,128)(2,1)S(1)}, bf16[2048,512]{1,0:T(8,128)(2,1)}, u32[]{:S(2)}) copy-start(bf16[2048,512]{1,0:T(8,128)(2,1)} %param.10) | copy-start | bytes 6291460
  7.2 133.3 %all-gather.2.cloned.1.call-start = ((), (), s32[]{:S(2)}) async-start(), calls=%async_computation.1 | async-start | bytes 2228224 | tf_op jit(solution)/shard_map/all_gather | solution.py:67
  9.0 219.6 %all-reduce.5.cloned.1.call-start = ((), (), s32[]{:S(2)}) async-start(), calls=%async_computation.3 | async-start | bytes 1048576 | tf_op jit(solution)/shard_map/psum | solution.py:74
  67.1 3.6 copy-start.5
  72.0 63.1 %collective-permute-start = (bf16[128,256,8]{1,0,2:T(8,128)(2,1)}, bf16[128,256,8]{1,0,2:T(8,128)(2,1)S(1)}, u32[]{:S(2)}, u32[]{:S(2)}) collective-permute-start(bf16[128,256,8]{1,0,2:T(8,128)(2,1)} %fusion.1), channel_id=1, source_target_pairs={{0,32},{32,64},{64,96},{96,128},{128,160},{160,192},{192,224},{224... | collective-permute-start | bytes 1572872 | tf_op jit(solution)/shard_map/ppermute | solution.py:16
  137.7 2.8 copy-start.2
  140.5 3.1 copy-start.7
  143.6 148.2 %reduce-scatter.2.cloned.1.call-start = ((), (), s32[]{:S(2)}) async-start(), calls=%async_computation.2 | async-start | bytes 2228224 | tf_op jit(solution)/shard_map/reduce_scatter | solution.py:78
  228.7 3.3 copy-start.4
  231.9 59.9 %copy-start.1 = (f32[128,512]{1,0:T(8,128)S(1)}, f32[128,512]{1,0:T(8,128)}, u32[]{:S(2)}) copy-start(f32[128,512]{1,0:T(8,128)} %param.11) | copy-start | bytes 786436
  231.9 102.5 %copy-start.6 = (f32[128,512]{1,0:T(8,128)S(1)}, f32[128,512]{1,0:T(8,128)}, u32[]{:S(2)}) copy-start(f32[128,512]{1,0:T(8,128)} %param.13) | copy-start | bytes 786436
  336.1 247.7 %copy-start.3 = (f32[128,512]{1,0:T(8,128)}, f32[128,512]{1,0:T(8,128)S(1)}, u32[]{:S(2)}) copy-start(f32[128,512]{1,0:T(8,128)S(1)} %get-tuple-element.11) | copy-start | bytes 786436
Sparse Core Ops, SparseCore 0:
  10.7 46.5 all-gather.1
  143.7 84.9 all-reduce.4
  232.0 59.6 reduce-scatter.1
